TPU v7x, 768 devices: a whole 4x8x12 slice. The times are simulated.
768 devices in a mesh: slab: 96 (over x, z, core), view: 8 (over y).
Axes of the slice: x: 4, y: 8, z: 12, core: 2. Of those that a mesh axis runs over, the one named last changes fastest.
Arguments:
- residual: bfloat16 [768, 192, 2, 128], P(('view', 'slab')), may hold values from -96 to 96
- route_list: int32 [768, 96, 2], P(('view', 'slab')), may hold values from -1 to 191, as said below
- tile_offsets: int32 [768], replicated, may hold values from 0 to 15
- view_geometry: float32 [4, 768], replicated, may hold values from 0 to 1
- line_coords: float32 [2, 1536, 128], P(None, 'slab'), may hold values from 0 to 1
- occupied: int32 [96, 8], P('slab'), may hold values from -1 to 15, as said below
- volume: float32 [1536, 128, 128], P('slab', 'view'), may hold values from -0.9 to 0.9
Outputs:
- new_volume: float32 [1536, 128, 128], P('slab', 'view')
Inputs may be any that keep to these rules, and one draw needn't show every extreme that they name: route_list[a, s, 0] is a block of view a's window that meets slab s; route_list[a, s, 1] is the block after it, or -1 where only one block meets the slab. Slab 96 - 1 receives two blocks from every view. The first entries of occupied[s] (one or more) are distinct bricks of slab s, numbered 0 to 15; the remaining entries are -1. Some slab lists 8 bricks, and some slab lists brick 16 - 1.
All inputs are finite; a program needn't handle non-finite values.
Results may differ from a plain program's by a relative error of at most 0.0034.
Values may be sent and summed in bfloat16 or wider, within the bound.
A program may use at most 32 MiB of HBM per device.

v0:
```python
import math

import jax
import jax.numpy as jnp
from jax import lax
from jax.sharding import PartitionSpec as P

relaxation = 0.9
damping = 0.1


def column_table(scales, offsets, columns):
    slopes = 0.8 + 0.05 * scales
    centre = (
        offsets.astype(jnp.float32)[:, None]
        + slopes[:, None] * jnp.arange(columns, dtype=jnp.float32)[None, :]
    )
    detector = jnp.arange(columns, dtype=jnp.float32)
    return jnp.maximum(0.0, 1.0 - jnp.abs(detector[None, :, None] - centre[:, None, :])).astype(
        jnp.bfloat16
    )


def line_hats(heights, depths, geometry, row_total):
    centre = 1.25 + 0.5 * geometry[0]
    tilt_rate = 0.6 + 0.6 * geometry[1]
    sweeps = 1.2 * geometry[2] - 0.6
    position = centre + tilt_rate * (heights[:, None] - 1.5) + sweeps * depths[:, None]
    levels = jnp.arange(row_total, dtype=jnp.float32)
    weight = jnp.maximum(0.0, 1.0 - jnp.abs(position[:, :, None] - levels))
    return weight.reshape(weight.shape[0], -1).astype(jnp.bfloat16)


def project_rows(stacked, scales, offsets):
    view_total = stacked.shape[0]
    group_size = math.gcd(view_total, 32)
    columns = stacked.shape[-1]

    def one_group(packed):
        rows_part, scale_part, offset_part = packed
        col_table = column_table(scale_part, offset_part, columns)
        return jnp.einsum(
            "vjc,vcx->vjx", rows_part, col_table, preferred_element_type=jnp.float32
        ).astype(jnp.bfloat16)

    groups = view_total // group_size
    shaped = (
        stacked.reshape((groups, group_size) + stacked.shape[1:]),
        scales.reshape(groups, group_size),
        offsets.reshape(groups, group_size),
    )
    result = lax.map(one_group, shaped)
    return result.reshape(stacked.shape)


def per_device(residual, route_list, tile_offsets, view_geometry, line_coords, occupied, volume):
    slab_count = lax.axis_size("slab")
    view_count = lax.axis_size("view")
    view_rank = lax.axis_index("view")
    total_views = slab_count * view_count
    window = residual[0]
    listed = route_list[0]
    present = listed >= 0
    picked = window[jnp.maximum(listed, 0)]
    picked = jnp.where(present[:, :, None, None], picked, jnp.zeros((), jnp.bfloat16))
    block_flags = present.astype(jnp.bfloat16)
    arrived, arrived_flags = (
        lax.all_to_all(picked, "slab", split_axis=0, concat_axis=0, tiled=True),
        lax.all_to_all(block_flags, "slab", split_axis=0, concat_axis=0, tiled=True),
    )
    tile_rows = arrived.shape[1] * arrived.shape[2]
    columns = arrived.shape[3]
    stacked = arrived.reshape(slab_count, tile_rows, columns)
    row_marks = jnp.repeat(arrived_flags, arrived.shape[2], axis=1)
    first_view = view_rank * slab_count
    group_geometry = lax.dynamic_slice_in_dim(view_geometry, first_view, slab_count, 1)
    group_offsets = lax.dynamic_slice_in_dim(tile_offsets, first_view, slab_count, 0)
    projected = project_rows(stacked, group_geometry[3], group_offsets)
    chosen = occupied[0]
    coords = line_coords[:, jnp.maximum(chosen, 0), :]
    heights = 3.0 * coords[0]
    depths = coords[1] - 0.5
    line_share = volume.shape[1]
    first_line = view_rank * line_share
    denom_shift = damping * total_views
    my_heights = lax.dynamic_slice_in_dim(heights, first_line, line_share, 1)
    my_depths = lax.dynamic_slice_in_dim(depths, first_line, line_share, 1)
    piece_rows = lax.all_gather(projected, "view", axis=0, tiled=True)
    piece_marks = lax.all_gather(row_marks, "view", axis=0, tiled=True)
    piece_flat = piece_rows.reshape(-1, columns)
    piece_mark = piece_marks.reshape(-1)

    def per_brick(packed):
        weights = line_hats(packed[0], packed[1], view_geometry, tile_rows)
        return (
            jnp.dot(weights, piece_flat, preferred_element_type=jnp.float32),
            jnp.dot(weights, piece_mark, preferred_element_type=jnp.float32),
        )

    numer_add, ray_add = lax.map(per_brick, (my_heights, my_depths))
    updates = relaxation * numer_add / (ray_add[..., None] + denom_shift)
    onehot = (chosen[None, :] == jnp.arange(volume.shape[0], dtype=jnp.int32)[:, None]).astype(
        jnp.float32
    )
    brick_add = jnp.einsum("bm,mrc->brc", onehot, updates, precision=lax.Precision.HIGHEST)
    return volume + brick_add


def solution(mesh):
    placed = (
        P(("view", "slab"), None, None, None),
        P(("view", "slab"), None, None),
        P(),
        P(),
        P(None, "slab", None),
        P("slab", None),
        P("slab", "view", None),
    )
    return jax.shard_map(
        per_device, mesh=mesh, in_specs=placed, out_specs=P("slab", "view", None), check_vma=False
    )
```

profile of v0, /device:TPU:6, one launch (start us, length us, event | category | flops | bytes accessed | tf_op | source)
XLA Modules:
  0.0 102.6 jit_solution(4701707971257731283)
XLA Ops:
  0.0 0.7 convert_bitcast_fusion
  0.7 0.7 copy.37
  1.5 19.4 %all-to-all-start.1 = ((bf16[96,1,2]{2,1,0:T(2,128)(2,1)}), bf16[96,1,2]{2,1,0:T(2,128)(2,1)S(1)}, u32[]{:S(2)}, u32[]{:S(2)}) async-start(bf16[96,1,2]{2,1,0:T(2,128)(2,1)} %copy.37), calls=%async_computation.1 | async-start | bytes 98304 | tf_op jit(solution)/shard_map/all_to_all | solution.py:69
  20.8 0.7 broadcast_maximum_fusion
  21.5 0.8 constant_dynamic-slice_fusion.4
  22.7 0.7 maximum_bitcast_fusion
  23.4 0.8 gather_fusion.1
  24.2 0.9 broadcast_select_fusion
  25.2 0.8 dynamic_slice.45
  26.0 1.3 %gather_fusion = f32[8,2,128]{2,0,1:T(8,128)S(1)} fusion(f32[2,16,128]{2,1,0:T(8,128)} %param.15, s32[1024]{0:T(1024)S(1)} %pad_clamp_fusion.1), kind=kCustom, calls=%fused_computation | custom fusion | bytes 16416 | tf_op jit(solution)/shard_map/gather | solution.py:80
  27.3 4.0 %all-to-all-done.1 = bf16[96,1,2]{2,1,0:T(2,128)(2,1)S(1)} async-done(((bf16[96,1,2]{2,1,0:T(2,128)(2,1)}), bf16[96,1,2]{2,1,0:T(2,128)(2,1)S(1)}, u32[]{:S(2)}, u32[]{:S(2)}) %all-to-all-start.1) | async-done | bytes 416 | tf_op jit(solution)/shard_map/all_to_all | solution.py:69
  31.3 9.3 %all-to-all-start = ((bf16[96,2,2,128]{3,2,1,0:T(2,128)(2,1)}), bf16[96,2,2,128]{3,2,1,0:T(2,128)(2,1)S(1)}, u32[]{:S(2)}, u32[]{:S(2)}) async-start(bf16[96,2,2,128]{3,2,1,0:T(2,128)(2,1)} %broadcast_select_fusion), calls=%async_computation | async-start | bytes 196608 | tf_op jit(solution)/shard_map/all_to_all | solution.py:68
  40.8 16.8 %all-gather = bf16[8,96,4]{1,2,0:T(4,128)(2,1)S(1)} all-gather(bf16[1,96,4]{1,2,0:T(4,128)(2,1)S(1)} %bitcast.76), channel_id=1, replica_groups=mesh['slab'=96,'view'=8] {'view'}, dimensions={0}, use_global_device_ids=true | all-gather | bytes 6912 | tf_op jit(solution)/shard_map/all_gather | solution.py:89
  57.5 0.2 copy.39
  57.7 0.2 reshape.233
  58.0 1.7 %while.24 = (s32[]{:T(128)}, bf16[3,32,4,128]{3,2,1,0:T(4,128)(2,1)S(1)}, bf16[3,32,4,128]{3,2,1,0:T(4,128)(2,1)S(1)}, s32[3,32]{1,0:T(4,128)S(1)}, f32[3,32]{1,0:T(4,128)S(1)}, /*index=5*/s32[]{:T(128)}) while((s32[]{:T(128)}, bf16[3,32,4,128]{3,2,1,0:T(4,128)(2,1)S(1)}, bf16[3,32,4,128]{3,2,1,0:T(4,128)(2,1)S(1)}, s32[3,32]{1,0:T(4,128)S(1)}, ...), condition=%wide.region_1.2_spmd, body=%wide.region_0.1_spmd.sunk | while | flops 6840418 | bytes 100173 | solution.py:52
  58.1 0.5 fusion.42
  58.7 0.5 fusion.42
  59.3 0.5 fusion.42
  59.7 26.1 %all_gather.6 = bf16[768,4,128]{2,1,0:T(4,128)(2,1)S(1)} all-gather(bf16[96,4,128]{2,1,0:T(4,128)(2,1)S(1)} %bitcast.73), channel_id=1, replica_groups=mesh['slab'=96,'view'=8] {'view'}, dimensions={0}, use_global_device_ids=true | all-gather | bytes 884736 | tf_op jit(solution)/shard_map/all_gather | solution.py:88
  85.8 15.6 %while.25 = (s32[]{:T(128)}, f32[8,16,128]{2,1,0:T(8,128)S(1)}, f32[8,16]{1,0:T(8,128)S(1)}, f32[4,768]{1,0:T(4,128)S(1)}, f32[8,16]{1,0:T(8,128)S(1)}, /*index=...) while((s32[]{:T(128)}, f32[8,16,128]{2,1,0:T(8,128)S(1)}, ...), condition=%wide.region_3.4_spmd, body=%wide.region_2.3_spmd.sunk | while | flops 12980754 | bytes 2463409 | solution.py:100
  86.1 0.3 sub.97
  86.4 0.2 sub.99
  86.7 0.5 maximum_convert_fusion.6
  87.1 0.3 fusion.48
  87.5 0.2 fusion.49
  88.1 0.3 sub.97
  88.4 0.2 sub.99
  88.6 0.5 maximum_convert_fusion.6
  89.1 0.3 fusion.48
  89.5 0.2 fusion.49
  89.9 0.2 copy.47
  90.0 0.3 sub.97
  90.3 0.2 sub.99
  90.6 0.5 maximum_convert_fusion.6
  91.0 0.3 fusion.48
  91.4 0.2 fusion.49
  92.0 0.3 sub.97
  92.3 0.2 sub.99
  92.5 0.5 maximum_convert_fusion.6
  93.0 0.3 fusion.48
  93.4 0.2 fusion.49
  93.9 0.3 sub.97
  94.3 0.2 sub.99
  94.5 0.5 maximum_convert_fusion.6
  95.0 0.3 fusion.48
  95.3 0.2 fusion.49
  95.9 0.3 sub.97
  96.2 0.2 sub.99
  96.4 0.5 maximum_convert_fusion.6
  96.9 0.3 fusion.48
  97.3 0.2 fusion.49
  97.8 0.3 sub.97
  98.2 0.2 sub.99
  98.4 0.5 maximum_convert_fusion.6
  98.9 0.3 fusion.48
  99.2 0.2 fusion.49
  99.8 0.3 sub.97
  100.1 0.2 sub.99
  100.3 0.5 maximum_convert_fusion.6
  100.8 0.3 fusion.48
  101.2 0.2 fusion.49
  101.6 0.3 convolution_add_fusion
  101.9 0.7 copy.42
  (90 shorter events, 3.9 us)
Async XLA Ops:
  0.0 23.3 %copy-start = (bf16[1,192,2,128]{3,2,1,0:T(2,128)(2,1)S(1)}, bf16[1,192,2,128]{3,2,1,0:T(2,128)(2,1)}, u32[]{:S(2)}) copy-start(bf16[1,192,2,128]{3,2,1,0:T(2,128)(2,1)} %param.11) | copy-start | bytes 294916
  1.5 29.9 %all-to-all-start.1 = ((bf16[96,1,2]{2,1,0:T(2,128)(2,1)}), bf16[96,1,2]{2,1,0:T(2,128)(2,1)S(1)}, u32[]{:S(2)}, u32[]{:S(2)}) async-start(bf16[96,1,2]{2,1,0:T(2,128)(2,1)} %copy.37), calls=%async_computation.1 | async-start | bytes 98304 | tf_op jit(solution)/shard_map/all_to_all | solution.py:69
  31.3 26.6 %all-to-all-start = ((bf16[96,2,2,128]{3,2,1,0:T(2,128)(2,1)}), bf16[96,2,2,128]{3,2,1,0:T(2,128)(2,1)S(1)}, u32[]{:S(2)}, u32[]{:S(2)}) async-start(bf16[96,2,2,128]{3,2,1,0:T(2,128)(2,1)} %broadcast_select_fusion), calls=%async_computation | async-start | bytes 196608 | tf_op jit(solution)/shard_map/all_to_all | solution.py:68
  58.0 27.8 %copy-start.1 = (f32[4,768]{1,0:T(4,128)S(1)}, f32[4,768]{1,0:T(4,128)}, u32[]{:S(2)}) copy-start(f32[4,768]{1,0:T(4,128)} %param.14) | copy-start | bytes 36868
  85.8 15.8 %copy-start.2 = (f32[16,16,128]{2,1,0:T(8,128)S(1)}, f32[16,16,128]{2,1,0:T(8,128)}, u32[]{:S(2)}) copy-start(f32[16,16,128]{2,1,0:T(8,128)} %param.17) | copy-start | bytes 393220
  85.8 15.8 %copy-start.3 = (s32[1,8]{1,0:T(1,128)S(1)}, s32[1,8]{1,0:T(1,128)}, u32[]{:S(2)}) copy-start(s32[1,8]{1,0:T(1,128)} %param.16) | copy-start | bytes 100
where the time goes:
time: 103 us
  blocking collectives  42.8 us (42%)
  starting transfers between devices  28.6 us (28%)
  local copies, waits for them, and re-layouts  12.1 us (12%)
  other arithmetic  8.14 us (8%)
  matrix products  6.15 us (6%)
  waiting for transfers between devices  4.02 us (4%)
    all_gather x1, blocking collectives, per_device(): piece_rows = lax.all_gather(projected, 'view', axis=0, tiled=True)  26.1 us
    all_to_all x1, starting transfers between devices, per_device(): lax.all_to_all(block_flags, 'slab', split_axis=0, concat_axis=0, tiled=True)  19.4 us
    all_gather x1, blocking collectives, per_device(): piece_marks = lax.all_gather(row_marks, 'view', axis=0, tiled=True)  16.8 us
    all_to_all x1, starting transfers between devices, per_device(): lax.all_to_all(picked, 'slab', split_axis=0, concat_axis=0, tiled=True)  9.25 us
    sub x24, local copies, waits for them, and re-layouts, line_hats(): weight = jnp.maximum(0.0, 1.0 - jnp.abs(position[:, :, None] - levels))  4.17 us
    all_to_all x1, waiting for transfers between devices, per_device(): lax.all_to_all(block_flags, 'slab', split_axis=0, concat_axis=0, tiled=True)  4.02 us
    convert_element_type x8, other arithmetic, line_hats(): return weight.reshape(weight.shape[0], -1).astype(jnp.bfloat16)  3.79 us
    dot_general x8, matrix products, per_brick(): jnp.dot(weights, piece_flat, preferred_element_type=jnp.float32)  2.75 us
  transfers between devices with their start and end apart: 2, of which 1 were waited for; matrix products, arithmetic and copies ran while one was open for 7% of the time, Pallas kernels for 0%

commit v1 on v0

v1 whole, which is shorter than its diff:
```python
import jax
import jax.numpy as jnp
from jax import lax
from jax.experimental import pallas as pl
from jax.experimental.pallas import tpu as pltpu
from jax.sharding import PartitionSpec as P

MESH = pl.DeviceIdType.MESH
F32 = jnp.float32
BF16 = jnp.bfloat16

NS = 96
NV = 8
VIEWS = 768
ROWS = 8
K = NS * ROWS
MB = 8
SHARE = 16
CHUNK = MB * SHARE
MSG = CHUNK + 16
RELAX = 0.9
SHIFT = 0.1 * VIEWS


def iota(shape, dim):
    return lax.broadcasted_iota(jnp.int32, shape, dim)


def drain(ref, sem):
    pltpu.make_async_copy(ref, ref, sem).wait()


def body(
    offs, occ, res, route, geo, lines, vol, out,
    snd, rcv, wgt, part, got, upd, ss, rs, ss2, rs2,
):
    s = lax.axis_index("slab")
    y = lax.axis_index("view")
    view = y * NS + s

    bar = pltpu.get_barrier_semaphore()

    def greet_slab(i, c):
        p = lax.rem(s + i, NS)
        pl.semaphore_signal(bar, inc=1, device_id=(p, y), device_id_type=MESH)
        return c

    lax.fori_loop(1, NS, greet_slab, 0)
    for d in range(1, NV):
        pl.semaphore_signal(bar, inc=1, device_id=(s, lax.rem(y + d, NV)), device_id_type=MESH)

    g = geo[...]
    lane = iota((4, VIEWS), 1)
    mine = jnp.sum(jnp.where(lane == view, g, 0.0), axis=1, keepdims=True)
    slope = 0.8 + 0.05 * mine[3:4, :]
    off = offs[view].astype(F32)
    col = iota((128, 128), 0).astype(F32)
    xs = iota((128, 128), 1).astype(F32)
    table = jnp.maximum(0.0, 1.0 - jnp.abs(col - (off + slope * xs))).astype(BF16)
    proj = jnp.dot(res[...], table, preferred_element_type=F32).astype(BF16)

    listed = route[0].astype(F32).astype(BF16)
    rr = iota((K, NS), 0)
    owner = (rr >> 3) == iota((K, NS), 1)
    spread = lax.dot_general(
        owner.astype(F32).astype(BF16), listed, (((1,), (1,)), ((), ())), preferred_element_type=F32
    )
    q = iota((K, 1), 0) & 7
    block = jnp.where((q & 2) == 0, spread[:, 0:1], spread[:, 1:2])
    want = jnp.where(q < 4, 2.0 * block + (q & 1).astype(F32), -1.0)
    pick = (iota((K, 384), 1).astype(F32) == want).astype(F32).astype(BF16)
    tile = jnp.dot(pick, proj, preferred_element_type=F32)
    mark = jnp.where((q >= 4) & (block >= 0.0), 1.0, 0.0)
    snd[...] = (tile + mark).astype(BF16).reshape(NS, ROWS, 128)

    pl.semaphore_wait(bar, NS - 1 + NV - 1)

    def send(i, c):
        p = lax.rem(s + i, NS)
        pltpu.make_async_remote_copy(
            src_ref=snd.at[p], dst_ref=rcv.at[s], send_sem=ss, recv_sem=rs,
            device_id=(p, y), device_id_type=MESH,
        ).start()
        return c

    lax.fori_loop(1, NS, send, 0)

    g1 = g.astype(BF16)
    r1 = g - g1.astype(F32)
    g2 = r1.astype(BF16)
    g3 = (r1 - g2.astype(F32)).astype(BF16)
    sel = (iota((VIEWS, K), 0) - y * NS) == (iota((VIEWS, K), 1) >> 3)
    sel = sel.astype(F32).astype(BF16)
    gg = (
        jnp.dot(g1, sel, preferred_element_type=F32)
        + jnp.dot(g2, sel, preferred_element_type=F32)
        + jnp.dot(g3, sel, preferred_element_type=F32)
    )
    centre = 1.25 + 0.5 * gg[0:1]
    tilt = 0.6 + 0.6 * gg[1:2]
    sweep = 1.2 * gg[2:3] - 0.6
    level = (iota((1, K), 1) & 3).astype(F32)
    hs = []
    ds = []
    for m in range(MB):
        brick = jnp.maximum(occ[0, m], 0)
        hs.append(3.0 * lines[0, pl.ds(brick, 1), :] - 1.5)
        ds.append(lines[1, pl.ds(brick, 1), :] - 0.5)
    hd = jnp.concatenate(hs + ds + [jnp.zeros((112, 128), F32)], axis=0)
    hdt = hd.T
    for d in range(NV):
        for m in range(MB):
            h = hdt[d * SHARE:(d + 1) * SHARE, m:m + 1]
            e = hdt[d * SHARE:(d + 1) * SHARE, MB + m:MB + m + 1]
            pos = centre + tilt * h + sweep * e
            w = jnp.maximum(0.0, 1.0 - jnp.abs(pos - level))
            wgt[pl.ds(d * CHUNK + m * SHARE, SHARE), :] = w.astype(BF16)

    drain(rcv.at[pl.ds(0, NS - 1)], rs)
    rcv[pl.ds(s, 1)] = snd[pl.ds(s, 1)]

    rows = rcv[...].reshape(K, 128)
    tiled = (iota((K, 128), 0) & 7) < 4
    zero = jnp.zeros((K, 128), BF16)
    both = jnp.concatenate([jnp.where(tiled, rows, zero), jnp.where(tiled, zero, rows)], axis=1)
    diag = iota((128, 128), 0) == iota((128, 128), 1)

    def chunk(d):
        r = jnp.dot(wgt[pl.ds(pl.multiple_of(d * CHUNK, CHUNK), CHUNK), :], both, preferred_element_type=F32)
        ray = jnp.sum(jnp.where(diag, r[:, 128:], 0.0), axis=0, keepdims=True)
        return r[:, :128], ray

    for d in (4, 3, 5, 2, 6, 1, 7):
        t = lax.rem(y + d, NV)
        num, ray = chunk(t)
        hi = ray.astype(BF16)
        lo = (ray - hi.astype(F32)).astype(BF16)
        part[t, 0:CHUNK, :] = num.astype(BF16)
        rowid = iota((16, 128), 0)
        hilo = jnp.where(rowid == 0, hi.astype(F32), jnp.where(rowid == 1, lo.astype(F32), 0.0))
        part[t, CHUNK:MSG, :] = hilo.astype(BF16)
        pltpu.make_async_remote_copy(
            src_ref=part.at[t], dst_ref=got.at[y], send_sem=ss2, recv_sem=rs2,
            device_id=(s, t), device_id_type=MESH,
        ).start()
    num, ray = chunk(y)
    got[pl.ds(y, 1)] = jnp.zeros((1, MSG, 128), BF16)
    drain(snd.at[pl.ds(0, NS - 1)], ss)
    drain(got.at[pl.ds(0, NV - 1)], rs2)
    for v in range(NV):
        num = num + got[v, 0:CHUNK, :].astype(F32)
        tail = got[v, CHUNK:MSG, :].astype(F32)
        ray = ray + (tail[0:1] + tail[1:2])
    rayc = jnp.broadcast_to(ray, (128, 128)).T
    new = RELAX * num / (rayc + SHIFT)
    upd[0:MB] = new.reshape(MB, SHARE, 128)
    upd[MB:MB + 1] = jnp.zeros((1, SHARE, 128), F32)
    for b in range(16):
        slot = jnp.int32(MB)
        for m in range(MB):
            slot = jnp.where(occ[0, m] == b, m, slot)
        out[b] = vol[b] + upd[slot]
    drain(part.at[pl.ds(0, NV - 1)], ss2)


def per_device(residual, route_list, tile_offsets, view_geometry, line_coords, occupied, volume):
    vm = pl.BlockSpec(memory_space=pltpu.VMEM)
    sm = pl.BlockSpec(memory_space=pltpu.SMEM)
    return pl.pallas_call(
        body,
        out_shape=jax.ShapeDtypeStruct(volume.shape, F32),
        in_specs=[sm, sm, vm, vm, vm, vm, vm],
        out_specs=vm,
        scratch_shapes=[
            pltpu.VMEM((NS, ROWS, 128), BF16),
            pltpu.VMEM((NS, ROWS, 128), BF16),
            pltpu.VMEM((NV * CHUNK, K), BF16),
            pltpu.VMEM((NV, MSG, 128), BF16),
            pltpu.VMEM((NV, MSG, 128), BF16),
            pltpu.VMEM((MB + 1, SHARE, 128), F32),
            pltpu.SemaphoreType.DMA,
            pltpu.SemaphoreType.DMA,
            pltpu.SemaphoreType.DMA,
            pltpu.SemaphoreType.DMA,
        ],
        compiler_params=pltpu.CompilerParams(
            collective_id=0, has_side_effects=True, vmem_limit_bytes=48 << 20
        ),
    )(
        tile_offsets, occupied, residual.reshape(384, 128), jnp.swapaxes(route_list, 1, 2), view_geometry,
        line_coords, volume,
    )


def solution(mesh):
    placed = (
        P(("view", "slab"), None, None, None),
        P(("view", "slab"), None, None),
        P(),
        P(),
        P(None, "slab", None),
        P("slab", None),
        P("slab", "view", None),
    )
    return jax.shard_map(
        per_device, mesh=mesh, in_specs=placed, out_specs=P("slab", "view", None), check_vma=False
    )
```

time: 103 us -> 46.9 us (0.46)
  the two profiles are of different devices: /device:TPU:6 before, /device:TPU:1 now
where the time goes in v1:
time: 46.9 us; the launch traced here: 46.6 us
  Pallas kernels  41.3 us (88%)
  local copies, waits for them, and re-layouts  5.24 us (11%)
    pallas_call x1, Pallas kernels, per_device(): pl.pallas_call(body, out_shape=jax.ShapeDtypeStruct(volume.shape, F32), i...  41.3 us
    unnamed x15, local copies, waits for them, and re-layouts  5.24 us

profile of v1, /device:TPU:1, one launch (start us, length us, event | category | flops | bytes accessed | tf_op | source)
XLA Modules:
  0.0 46.6 jit_solution(2326366549221962300)
XLA Ops:
  0.0 0.0 copy-start.5
  0.0 0.0 copy-start.6
  0.0 0.7 %copy-done.5 = s32[1,96,2]{1,2,0:T(2,128)S(1)} copy-done((s32[1,96,2]{1,2,0:T(2,128)S(1)}, s32[1,96,2]{1,2,0:T(2,128)}, u32[]{:S(2)}) %copy-start.5) | copy-done | bytes 792
  0.7 0.0 copy-done.6
  0.7 0.0 copy-start
  0.7 0.9 %copy-done = f32[16,16,128]{2,1,0:T(8,128)S(1)} copy-done((f32[16,16,128]{2,1,0:T(8,128)S(1)}, f32[16,16,128]{2,1,0:T(8,128)}, u32[]{:S(2)}) %copy-start) | copy-done | bytes 131096
  1.6 0.0 copy-start.1
  1.6 0.9 %copy-done.1 = bf16[1,192,2,128]{3,2,1,0:T(2,128)(2,1)S(1)} copy-done((bf16[1,192,2,128]{3,2,1,0:T(2,128)(2,1)S(1)}, bf16[1,192,2,128]{3,2,1,0:T(2,128)(2,1)}, u32[]{:S(2)}) %copy-start.1) | copy-done | bytes 98328
  2.5 0.0 copy-start.2
  2.5 0.7 %copy-done.2 = f32[2,16,128]{2,1,0:T(8,128)S(1)} copy-done((f32[2,16,128]{2,1,0:T(8,128)S(1)}, f32[2,16,128]{2,1,0:T(8,128)}, u32[]{:S(2)}) %copy-start.2) | copy-done | bytes 16408
  3.2 0.0 copy-start.3
  3.2 0.7 %copy-done.3 = f32[4,768]{1,0:T(4,128)S(1)} copy-done((f32[4,768]{1,0:T(4,128)S(1)}, f32[4,768]{1,0:T(4,128)}, u32[]{:S(2)}) %copy-start.3) | copy-done | bytes 12312
  3.9 0.0 copy-start.4
  3.9 0.7 %copy-done.4 = s32[768]{0:T(1024)S(1)} copy-done((s32[768]{0:T(1024)S(1)}, s32[768]{0:T(1024)}, u32[]{:S(2)}) %copy-start.4) | copy-done | bytes 3096
  4.6 41.3 %shard_map.73 = f32[16,16,128]{2,1,0:T(8,128)S(1)} custom-call(s32[768]{0:T(1024)S(1)} %copy-done.4, s32[1,8]{1,0:T(1,128)S(1)} %copy-done.6, bf16[384,128]{1,0:T(8,128)(2,1)S(1)} %bitcast.2, s32[1,2,96]{2,1,0:T(2,128)S(1)} %bitcast.3, f32[4,768]{1,0:T(4,128)S(1)} %copy-done.3, f32[2,16,128]{2,1,0:T(8,128)S(1)} %copy-done.2, f32[16,16,128]{2,1,0:T(8,128)S(1)} %copy-done), custom_call_target="tpu_custom_call" | custom-call | tf_op jit(solution)/shard_map/pallas_call | solution.py:169
  45.9 0.7 %copy.9 = f32[16,16,128]{2,1,0:T(8,128)} copy(f32[16,16,128]{2,1,0:T(8,128)S(1)} %shard_map.73) | data formatting | bytes 262144
Async XLA Ops:
  0.0 0.7 %copy-start.5 = (s32[1,96,2]{1,2,0:T(2,128)S(1)}, s32[1,96,2]{1,2,0:T(2,128)}, u32[]{:S(2)}) copy-start(s32[1,96,2]{1,2,0:T(2,128)} %param.8) | copy-start | bytes 2308
  0.0 0.7 %copy-start.6 = (s32[1,8]{1,0:T(1,128)S(1)}, s32[1,8]{1,0:T(1,128)}, u32[]{:S(2)}) copy-start(s32[1,8]{1,0:T(1,128)} %occ.1) | copy-start | bytes 100
  0.7 0.9 %copy-start = (f32[16,16,128]{2,1,0:T(8,128)S(1)}, f32[16,16,128]{2,1,0:T(8,128)}, u32[]{:S(2)}) copy-start(f32[16,16,128]{2,1,0:T(8,128)} %vol.1) | copy-start | bytes 393220
  1.6 0.9 %copy-start.1 = (bf16[1,192,2,128]{3,2,1,0:T(2,128)(2,1)S(1)}, bf16[1,192,2,128]{3,2,1,0:T(2,128)(2,1)}, u32[]{:S(2)}) copy-start(bf16[1,192,2,128]{3,2,1,0:T(2,128)(2,1)} %param.7) | copy-start | bytes 294916
  2.5 0.7 %copy-start.2 = (f32[2,16,128]{2,1,0:T(8,128)S(1)}, f32[2,16,128]{2,1,0:T(8,128)}, u32[]{:S(2)}) copy-start(f32[2,16,128]{2,1,0:T(8,128)} %lines.1) | copy-start | bytes 49156
  3.2 0.7 %copy-start.3 = (f32[4,768]{1,0:T(4,128)S(1)}, f32[4,768]{1,0:T(4,128)}, u32[]{:S(2)}) copy-start(f32[4,768]{1,0:T(4,128)} %geo.1) | copy-start | bytes 36868
  3.9 0.7 %copy-start.4 = (s32[768]{0:T(1024)S(1)}, s32[768]{0:T(1024)}, u32[]{:S(2)}) copy-start(s32[768]{0:T(1024)} %offs.1) | copy-start | bytes 9220

commit v2 on v1

--- a/solution.py
+++ b/solution.py
@@ -12,7 +12,7 @@
 NS = 96
 NV = 8
 VIEWS = 768
-ROWS = 8
+ROWS = 4
 K = NS * ROWS
 MB = 8
 SHARE = 16
@@ -30,25 +30,61 @@
     pltpu.make_async_copy(ref, ref, sem).wait()
 
 
+def ring(v, step, n):
+    t = v + step
+    return jnp.where(t >= n, t - n, t)
+
+
+def peers(s, act):
+    x = s // 24
+    z = (s - 24 * x) >> 1
+    c = s & 1
+    bases = [24 * ((x + dx) & 3) + (c ^ dc) for dx in (2, 1, 3, 0) for dc in (1, 0)]
+
+    def column(i, carry):
+        dz = jnp.where(i >= 6, i - 5, i + 6)
+        t = 2 * ring(z, dz, 12)
+        for base in bases:
+            act(base + t)
+        return carry
+
+    lax.fori_loop(0, 11, column, 0)
+    for base in bases[:-1]:
+        act(base + 2 * z)
+
+
 def body(
-    offs, occ, res, route, geo, lines, vol, out,
-    snd, rcv, wgt, part, got, upd, ss, rs, ss2, rs2,
+    offs_h, occ_h, res_h, route_h, geo_h, lines_h, vol_h, out,
+    offs, occ, res, route, geo, lines, vol,
+    snd, rcv, msnd, mrcv, wgt, part, got, upd, ins, ss, rs, ms, mr, ss2, rs2,
 ):
     s = lax.axis_index("slab")
     y = lax.axis_index("view")
     view = y * NS + s
 
+    fetch = [
+        pltpu.make_async_copy(h, v, ins.at[i])
+        for i, (h, v) in enumerate(
+            [
+                (res_h, res), (route_h, route), (geo_h, geo), (offs_h, offs),
+                (occ_h, occ), (lines_h, lines), (vol_h, vol),
+            ]
+        )
+    ]
+    for f in fetch:
+        f.start()
+
     bar = pltpu.get_barrier_semaphore()
 
-    def greet_slab(i, c):
-        p = lax.rem(s + i, NS)
+    def greet(p):
         pl.semaphore_signal(bar, inc=1, device_id=(p, y), device_id_type=MESH)
-        return c
-
-    lax.fori_loop(1, NS, greet_slab, 0)
+
+    peers(s, greet)
     for d in range(1, NV):
-        pl.semaphore_signal(bar, inc=1, device_id=(s, lax.rem(y + d, NV)), device_id_type=MESH)
-
+        pl.semaphore_signal(bar, inc=1, device_id=(s, (y + d) & 7), device_id_type=MESH)
+
+    for f in fetch[:4]:
+        f.wait()
     g = geo[...]
     lane = iota((4, VIEWS), 1)
     mine = jnp.sum(jnp.where(lane == view, g, 0.0), axis=1, keepdims=True)
@@ -59,37 +95,43 @@
     table = jnp.maximum(0.0, 1.0 - jnp.abs(col - (off + slope * xs))).astype(BF16)
     proj = jnp.dot(res[...], table, preferred_element_type=F32).astype(BF16)
 
-    listed = route[0].astype(F32).astype(BF16)
-    rr = iota((K, NS), 0)
-    owner = (rr >> 3) == iota((K, NS), 1)
+    blocks = route[0].astype(F32)
+    listed = blocks.astype(BF16)
+    owner = (iota((K, NS), 0) >> 2) == iota((K, NS), 1)
     spread = lax.dot_general(
         owner.astype(F32).astype(BF16), listed, (((1,), (1,)), ((), ())), preferred_element_type=F32
     )
-    q = iota((K, 1), 0) & 7
-    block = jnp.where((q & 2) == 0, spread[:, 0:1], spread[:, 1:2])
-    want = jnp.where(q < 4, 2.0 * block + (q & 1).astype(F32), -1.0)
+    q = iota((K, 1), 0) & 3
+    block = jnp.where(q < 2, spread[:, 0:1], spread[:, 1:2])
+    want = 2.0 * block + (q & 1).astype(F32)
     pick = (iota((K, 384), 1).astype(F32) == want).astype(F32).astype(BF16)
     tile = jnp.dot(pick, proj, preferred_element_type=F32)
-    mark = jnp.where((q >= 4) & (block >= 0.0), 1.0, 0.0)
-    snd[...] = (tile + mark).astype(BF16).reshape(NS, ROWS, 128)
+    snd[...] = tile.astype(BF16).reshape(NS, ROWS, 128)
+    flags = jnp.where(blocks >= 0.0, 1.0, 0.0)
+    flags = jnp.concatenate([flags, jnp.zeros((2, 128 - NS), F32)], axis=1)
+    msnd[...] = flags.astype(BF16).reshape(1, 2, 128)
 
     pl.semaphore_wait(bar, NS - 1 + NV - 1)
 
-    def send(i, c):
-        p = lax.rem(s + i, NS)
+    def send(p):
+        pltpu.make_async_remote_copy(
+            src_ref=msnd.at[0], dst_ref=mrcv.at[s], send_sem=ms, recv_sem=mr,
+            device_id=(p, y), device_id_type=MESH,
+        ).start()
         pltpu.make_async_remote_copy(
             src_ref=snd.at[p], dst_ref=rcv.at[s], send_sem=ss, recv_sem=rs,
             device_id=(p, y), device_id_type=MESH,
         ).start()
-        return c
-
-    lax.fori_loop(1, NS, send, 0)
-
+
+    peers(s, send)
+
+    for f in fetch[4:6]:
+        f.wait()
     g1 = g.astype(BF16)
     r1 = g - g1.astype(F32)
     g2 = r1.astype(BF16)
     g3 = (r1 - g2.astype(F32)).astype(BF16)
-    sel = (iota((VIEWS, K), 0) - y * NS) == (iota((VIEWS, K), 1) >> 3)
+    sel = (iota((VIEWS, K), 0) - y * NS) == (iota((VIEWS, K), 1) >> 2)
     sel = sel.astype(F32).astype(BF16)
     gg = (
         jnp.dot(g1, sel, preferred_element_type=F32)
@@ -116,13 +158,16 @@
             w = jnp.maximum(0.0, 1.0 - jnp.abs(pos - level))
             wgt[pl.ds(d * CHUNK + m * SHARE, SHARE), :] = w.astype(BF16)
 
+    drain(mrcv.at[pl.ds(0, NS - 1)], mr)
+    mrcv[pl.ds(s, 1)] = msnd[...]
+    here = (iota((128, 128), 0) == s).astype(F32).astype(BF16)
+    marks = jnp.dot(mrcv[...].reshape(2 * NS, 128), here, preferred_element_type=F32).astype(BF16)
+    twice = ((iota((K, 2 * NS), 0) >> 1) == iota((K, 2 * NS), 1)).astype(F32).astype(BF16)
+    marks = jnp.dot(twice, marks, preferred_element_type=F32).astype(BF16)
+
     drain(rcv.at[pl.ds(0, NS - 1)], rs)
     rcv[pl.ds(s, 1)] = snd[pl.ds(s, 1)]
-
-    rows = rcv[...].reshape(K, 128)
-    tiled = (iota((K, 128), 0) & 7) < 4
-    zero = jnp.zeros((K, 128), BF16)
-    both = jnp.concatenate([jnp.where(tiled, rows, zero), jnp.where(tiled, zero, rows)], axis=1)
+    both = jnp.concatenate([rcv[...].reshape(K, 128), marks], axis=1)
     diag = iota((128, 128), 0) == iota((128, 128), 1)
 
     def chunk(d):
@@ -130,13 +175,13 @@
         ray = jnp.sum(jnp.where(diag, r[:, 128:], 0.0), axis=0, keepdims=True)
         return r[:, :128], ray
 
+    rowid = iota((16, 128), 0)
     for d in (4, 3, 5, 2, 6, 1, 7):
-        t = lax.rem(y + d, NV)
+        t = (y + d) & 7
         num, ray = chunk(t)
         hi = ray.astype(BF16)
         lo = (ray - hi.astype(F32)).astype(BF16)
         part[t, 0:CHUNK, :] = num.astype(BF16)
-        rowid = iota((16, 128), 0)
         hilo = jnp.where(rowid == 0, hi.astype(F32), jnp.where(rowid == 1, lo.astype(F32), 0.0))
         part[t, CHUNK:MSG, :] = hilo.astype(BF16)
         pltpu.make_async_remote_copy(
@@ -145,7 +190,9 @@
         ).start()
     num, ray = chunk(y)
     got[pl.ds(y, 1)] = jnp.zeros((1, MSG, 128), BF16)
+    fetch[6].wait()
     drain(snd.at[pl.ds(0, NS - 1)], ss)
+    drain(mrcv.at[pl.ds(0, NS - 1)], ms)
     drain(got.at[pl.ds(0, NV - 1)], rs2)
     for v in range(NV):
         num = num + got[v, 0:CHUNK, :].astype(F32)
@@ -164,31 +211,37 @@
 
 
 def per_device(residual, route_list, tile_offsets, view_geometry, line_coords, occupied, volume):
-    vm = pl.BlockSpec(memory_space=pltpu.VMEM)
-    sm = pl.BlockSpec(memory_space=pltpu.SMEM)
+    hbm = pl.BlockSpec(memory_space=pltpu.HBM)
+    sem = pltpu.SemaphoreType.DMA
     return pl.pallas_call(
         body,
         out_shape=jax.ShapeDtypeStruct(volume.shape, F32),
-        in_specs=[sm, sm, vm, vm, vm, vm, vm],
-        out_specs=vm,
+        in_specs=[hbm] * 7,
+        out_specs=pl.BlockSpec(memory_space=pltpu.VMEM),
         scratch_shapes=[
+            pltpu.SMEM((VIEWS,), jnp.int32),
+            pltpu.SMEM((1, MB), jnp.int32),
+            pltpu.VMEM((384, 128), BF16),
+            pltpu.VMEM((1, 2, NS), jnp.int32),
+            pltpu.VMEM((4, VIEWS), F32),
+            pltpu.VMEM((2, 16, 128), F32),
+            pltpu.VMEM((16, SHARE, 128), F32),
             pltpu.VMEM((NS, ROWS, 128), BF16),
             pltpu.VMEM((NS, ROWS, 128), BF16),
+            pltpu.VMEM((1, 2, 128), BF16),
+            pltpu.VMEM((NS, 2, 128), BF16),
             pltpu.VMEM((NV * CHUNK, K), BF16),
             pltpu.VMEM((NV, MSG, 128), BF16),
             pltpu.VMEM((NV, MSG, 128), BF16),
             pltpu.VMEM((MB + 1, SHARE, 128), F32),
-            pltpu.SemaphoreType.DMA,
-            pltpu.SemaphoreType.DMA,
-            pltpu.SemaphoreType.DMA,
-            pltpu.SemaphoreType.DMA,
+            sem((7,)), sem, sem, sem, sem, sem, sem,
         ],
         compiler_params=pltpu.CompilerParams(
-            collective_id=0, has_side_effects=True, vmem_limit_bytes=48 << 20
+            collective_id=0, has_side_effects=True, vmem_limit_bytes=60 << 20
         ),
     )(
-        tile_offsets, occupied, residual.reshape(384, 128), jnp.swapaxes(route_list, 1, 2), view_geometry,
-        line_coords, volume,
+        tile_offsets, occupied, residual.reshape(384, 128), jnp.swapaxes(route_list, 1, 2),
+        view_geometry, line_coords, volume,
     )
 
 

time: 46.9 us -> 41.4 us (0.88)
  local copies, waits for them, and re-layouts: 5.24 us -> 1.57 us
  Pallas kernels: 41.3 us -> 39.7 us
    unnamed x15 -> x1, local copies, waits for them, and re-layouts: 5.24 us -> 1.57 us
    pallas_call x1, Pallas kernels: 41.3 us -> 39.7 us  [per_device(): pl.pallas_call(body, out_shape=jax.ShapeDtypeStruct(volume.shape, F32), i...]
where the time goes in v2:
time: 41.4 us; the launch traced here: 41.3 us
  Pallas kernels  39.7 us (96%)
  local copies, waits for them, and re-layouts  1.57 us (4%)
    pallas_call x1, Pallas kernels, per_device(): pl.pallas_call(body, out_shape=jax.ShapeDtypeStruct(volume.shape, F32), i...  39.7 us
    unnamed x1, local copies, waits for them, and re-layouts  1.57 us

profile of v2, /device:TPU:1, one launch (start us, length us, event | category | flops | bytes accessed | tf_op | source)
XLA Modules:
  0.0 41.3 jit_solution(15581190542338562846)
XLA Ops:
  0.0 39.7 %shard_map.73 = f32[16,16,128]{2,1,0:T(8,128)} custom-call(s32[768]{0:T(1024)} %offs_h.1, s32[1,8]{1,0:T(1,128)} %occ_h.1, bf16[384,128]{1,0:T(8,128)(2,1)} %bitcast.2, s32[1,2,96]{2,1,0:T(2,128)} %bitcast.3, f32[4,768]{1,0:T(4,128)} %geo_h.1, f32[2,16,128]{2,1,0:T(8,128)} %lines_h.1, f32[16,16,128]{2,1,0:T(8,128)} %vol_h.1), custom_call_target="tpu_custom_call" | custom-call | tf_op jit(solution)/shard_map/pallas_call | solution.py:216
  39.7 1.6 %copy.9 = f32[16,16,128]{2,1,0:T(8,128)} copy(f32[16,16,128]{2,1,0:T(8,128)} %shard_map.73) | data formatting | bytes 262144

commit v3 on v2

--- a/solution.py
+++ b/solution.py
@@ -17,7 +17,6 @@
 MB = 8
 SHARE = 16
 CHUNK = MB * SHARE
-MSG = CHUNK + 16
 RELAX = 0.9
 SHIFT = 0.1 * VIEWS
 
@@ -56,11 +55,15 @@
 def body(
     offs_h, occ_h, res_h, route_h, geo_h, lines_h, vol_h, out,
     offs, occ, res, route, geo, lines, vol,
-    snd, rcv, msnd, mrcv, wgt, part, got, upd, ins, ss, rs, ms, mr, ss2, rs2,
+    snd, rcv, mrcv, wgt, part, got, rpart, rgot, upd, ins, ss, rs, ms, mr, ms2, mr2, ss2, rs2, ss3, rs3,
 ):
     s = lax.axis_index("slab")
     y = lax.axis_index("view")
     view = y * NS + s
+    x = s // 24
+    z = (s - 24 * x) >> 1
+    core = s & 1
+    k = 2 * x + core
 
     fetch = [
         pltpu.make_async_copy(h, v, ins.at[i])
@@ -109,15 +112,22 @@
     snd[...] = tile.astype(BF16).reshape(NS, ROWS, 128)
     flags = jnp.where(blocks >= 0.0, 1.0, 0.0)
     flags = jnp.concatenate([flags, jnp.zeros((2, 128 - NS), F32)], axis=1)
-    msnd[...] = flags.astype(BF16).reshape(1, 2, 128)
+    mrcv[pl.ds(k, 1), pl.ds(z, 1)] = flags.astype(BF16).reshape(1, 1, 2, 128)
 
     pl.semaphore_wait(bar, NS - 1 + NV - 1)
 
+    def send_marks(i, c):
+        dz = jnp.where(i >= 6, i - 5, i + 6)
+        t = ring(z, dz, 12)
+        pltpu.make_async_remote_copy(
+            src_ref=mrcv.at[k, z], dst_ref=mrcv.at[k, z], send_sem=ms, recv_sem=mr,
+            device_id=(24 * x + 2 * t + core, y), device_id_type=MESH,
+        ).start()
+        return c
+
+    lax.fori_loop(0, 11, send_marks, 0)
+
     def send(p):
-        pltpu.make_async_remote_copy(
-            src_ref=msnd.at[0], dst_ref=mrcv.at[s], send_sem=ms, recv_sem=mr,
-            device_id=(p, y), device_id_type=MESH,
-        ).start()
         pltpu.make_async_remote_copy(
             src_ref=snd.at[p], dst_ref=rcv.at[s], send_sem=ss, recv_sem=rs,
             device_id=(p, y), device_id_type=MESH,
@@ -142,6 +152,15 @@
     tilt = 0.6 + 0.6 * gg[1:2]
     sweep = 1.2 * gg[2:3] - 0.6
     level = (iota((1, K), 1) & 3).astype(F32)
+    def forward_marks():
+        drain(mrcv.at[0, pl.ds(0, 11)], mr)
+        for dx, dc in ((2, 1), (2, 0), (1, 1), (3, 1), (1, 0), (3, 0), (0, 1)):
+            p = 24 * ((x + dx) & 3) + 2 * z + (core ^ dc)
+            pltpu.make_async_remote_copy(
+                src_ref=mrcv.at[k], dst_ref=mrcv.at[k], send_sem=ms2, recv_sem=mr2,
+                device_id=(p, y), device_id_type=MESH,
+            ).start()
+
     hs = []
     ds = []
     for m in range(MB):
@@ -157,12 +176,16 @@
             pos = centre + tilt * h + sweep * e
             w = jnp.maximum(0.0, 1.0 - jnp.abs(pos - level))
             wgt[pl.ds(d * CHUNK + m * SHARE, SHARE), :] = w.astype(BF16)
-
-    drain(mrcv.at[pl.ds(0, NS - 1)], mr)
-    mrcv[pl.ds(s, 1)] = msnd[...]
+    forward_marks()
+
+    drain(mrcv.at[pl.ds(0, 7)], mr2)
     here = (iota((128, 128), 0) == s).astype(F32).astype(BF16)
     marks = jnp.dot(mrcv[...].reshape(2 * NS, 128), here, preferred_element_type=F32).astype(BF16)
-    twice = ((iota((K, 2 * NS), 0) >> 1) == iota((K, 2 * NS), 1)).astype(F32).astype(BF16)
+    r = iota((K, 1), 0)
+    a = r >> 2
+    xa = (a >= 24).astype(jnp.int32) + (a >= 48).astype(jnp.int32) + (a >= 72).astype(jnp.int32)
+    place = 24 * (2 * xa + (a & 1)) + 2 * ((a - 24 * xa) >> 1) + ((r >> 1) & 1)
+    twice = (place == iota((K, 2 * NS), 1)).astype(F32).astype(BF16)
     marks = jnp.dot(twice, marks, preferred_element_type=F32).astype(BF16)
 
     drain(rcv.at[pl.ds(0, NS - 1)], rs)
@@ -175,28 +198,34 @@
         ray = jnp.sum(jnp.where(diag, r[:, 128:], 0.0), axis=0, keepdims=True)
         return r[:, :128], ray
 
-    rowid = iota((16, 128), 0)
     for d in (4, 3, 5, 2, 6, 1, 7):
         t = (y + d) & 7
         num, ray = chunk(t)
         hi = ray.astype(BF16)
         lo = (ray - hi.astype(F32)).astype(BF16)
-        part[t, 0:CHUNK, :] = num.astype(BF16)
-        hilo = jnp.where(rowid == 0, hi.astype(F32), jnp.where(rowid == 1, lo.astype(F32), 0.0))
-        part[t, CHUNK:MSG, :] = hilo.astype(BF16)
+        part[t] = num.astype(BF16)
+        hilo = jnp.concatenate([hi.astype(F32), lo.astype(F32)], axis=0)
+        rpart[pl.ds(t, 1)] = hilo.astype(BF16).reshape(1, 2, 128)
         pltpu.make_async_remote_copy(
             src_ref=part.at[t], dst_ref=got.at[y], send_sem=ss2, recv_sem=rs2,
             device_id=(s, t), device_id_type=MESH,
         ).start()
+        pltpu.make_async_remote_copy(
+            src_ref=rpart.at[t], dst_ref=rgot.at[y], send_sem=ss3, recv_sem=rs3,
+            device_id=(s, t), device_id_type=MESH,
+        ).start()
     num, ray = chunk(y)
-    got[pl.ds(y, 1)] = jnp.zeros((1, MSG, 128), BF16)
+    got[pl.ds(y, 1)] = jnp.zeros((1, CHUNK, 128), BF16)
+    rgot[pl.ds(y, 1)] = jnp.zeros((1, 2, 128), BF16)
     fetch[6].wait()
     drain(snd.at[pl.ds(0, NS - 1)], ss)
-    drain(mrcv.at[pl.ds(0, NS - 1)], ms)
+    drain(mrcv.at[0, pl.ds(0, 11)], ms)
+    drain(mrcv.at[pl.ds(0, 7)], ms2)
+    drain(rgot.at[pl.ds(0, NV - 1)], rs3)
     drain(got.at[pl.ds(0, NV - 1)], rs2)
     for v in range(NV):
-        num = num + got[v, 0:CHUNK, :].astype(F32)
-        tail = got[v, CHUNK:MSG, :].astype(F32)
+        num = num + got[v].astype(F32)
+        tail = rgot[v].astype(F32)
         ray = ray + (tail[0:1] + tail[1:2])
     rayc = jnp.broadcast_to(ray, (128, 128)).T
     new = RELAX * num / (rayc + SHIFT)
@@ -208,6 +237,7 @@
             slot = jnp.where(occ[0, m] == b, m, slot)
         out[b] = vol[b] + upd[slot]
     drain(part.at[pl.ds(0, NV - 1)], ss2)
+    drain(rpart.at[pl.ds(0, NV - 1)], ss3)
 
 
 def per_device(residual, route_list, tile_offsets, view_geometry, line_coords, occupied, volume):
@@ -228,13 +258,14 @@
             pltpu.VMEM((16, SHARE, 128), F32),
             pltpu.VMEM((NS, ROWS, 128), BF16),
             pltpu.VMEM((NS, ROWS, 128), BF16),
-            pltpu.VMEM((1, 2, 128), BF16),
-            pltpu.VMEM((NS, 2, 128), BF16),
+            pltpu.VMEM((8, 12, 2, 128), BF16),
             pltpu.VMEM((NV * CHUNK, K), BF16),
-            pltpu.VMEM((NV, MSG, 128), BF16),
-            pltpu.VMEM((NV, MSG, 128), BF16),
+            pltpu.VMEM((NV, CHUNK, 128), BF16),
+            pltpu.VMEM((NV, CHUNK, 128), BF16),
+            pltpu.VMEM((NV, 2, 128), BF16),
+            pltpu.VMEM((NV, 2, 128), BF16),
             pltpu.VMEM((MB + 1, SHARE, 128), F32),
-            sem((7,)), sem, sem, sem, sem, sem, sem,
+            sem((7,)), sem, sem, sem, sem, sem, sem, sem, sem, sem, sem,
         ],
         compiler_params=pltpu.CompilerParams(
             collective_id=0, has_side_effects=True, vmem_limit_bytes=60 << 20

time: 41.4 us -> 40 us (0.966)
  Pallas kernels: 39.7 us -> 38.3 us
    pallas_call x1, Pallas kernels: 39.7 us -> 38.3 us  [per_device(): pl.pallas_call(body, out_shape=jax.ShapeDtypeStruct(volume.shape, F32), i...]
where the time goes in v3:
time: 40 us; the launch traced here: 39.9 us
  Pallas kernels  38.3 us (96%)
  local copies, waits for them, and re-layouts  1.57 us (4%)
    pallas_call x1, Pallas kernels, per_device(): pl.pallas_call(body, out_shape=jax.ShapeDtypeStruct(volume.shape, F32), i...  38.3 us
    unnamed x1, local copies, waits for them, and re-layouts  1.57 us

profile of v3, /device:TPU:1, one launch (start us, length us, event | category | flops | bytes accessed | tf_op | source)
XLA Modules:
  0.0 39.9 jit_solution(5031966674586823249)
XLA Ops:
  0.0 38.3 %shard_map.73 = f32[16,16,128]{2,1,0:T(8,128)} custom-call(s32[768]{0:T(1024)} %offs_h.1, s32[1,8]{1,0:T(1,128)} %occ_h.1, bf16[384,128]{1,0:T(8,128)(2,1)} %bitcast.2, s32[1,2,96]{2,1,0:T(2,128)} %bitcast.3, f32[4,768]{1,0:T(4,128)} %geo_h.1, f32[2,16,128]{2,1,0:T(8,128)} %lines_h.1, f32[16,16,128]{2,1,0:T(8,128)} %vol_h.1), custom_call_target="tpu_custom_call" | custom-call | tf_op jit(solution)/shard_map/pallas_call | solution.py:246
  38.3 1.6 %copy.9 = f32[16,16,128]{2,1,0:T(8,128)} copy(f32[16,16,128]{2,1,0:T(8,128)} %shard_map.73) | data formatting | bytes 262144

commit v4 on v3

--- a/solution.py
+++ b/solution.py
@@ -74,8 +74,8 @@
             ]
         )
     ]
-    for f in fetch:
-        f.start()
+    for i in (1, 0, 2, 3, 4, 5, 6):
+        fetch[i].start()
 
     bar = pltpu.get_barrier_semaphore()
 
@@ -86,8 +86,23 @@
     for d in range(1, NV):
         pl.semaphore_signal(bar, inc=1, device_id=(s, (y + d) & 7), device_id_type=MESH)
 
-    for f in fetch[:4]:
-        f.wait()
+    fetch[1].wait()
+    blocks = route[0].astype(F32)
+    listed = blocks.astype(BF16)
+    owner = (iota((K, NS), 0) >> 2) == iota((K, NS), 1)
+    spread = lax.dot_general(
+        owner.astype(F32).astype(BF16), listed, (((1,), (1,)), ((), ())), preferred_element_type=F32
+    )
+    q = iota((K, 1), 0) & 3
+    block = jnp.where(q < 2, spread[:, 0:1], spread[:, 1:2])
+    want = 2.0 * block + (q & 1).astype(F32)
+    pick = (iota((K, 384), 1).astype(F32) == want).astype(F32).astype(BF16)
+    flags = jnp.where(blocks >= 0.0, 1.0, 0.0)
+    flags = jnp.concatenate([flags, jnp.zeros((2, 128 - NS), F32)], axis=1)
+    mrcv[pl.ds(k, 1), pl.ds(z, 1)] = flags.astype(BF16).reshape(1, 1, 2, 128)
+
+    fetch[2].wait()
+    fetch[3].wait()
     g = geo[...]
     lane = iota((4, VIEWS), 1)
     mine = jnp.sum(jnp.where(lane == view, g, 0.0), axis=1, keepdims=True)
@@ -96,23 +111,10 @@
     col = iota((128, 128), 0).astype(F32)
     xs = iota((128, 128), 1).astype(F32)
     table = jnp.maximum(0.0, 1.0 - jnp.abs(col - (off + slope * xs))).astype(BF16)
+    fetch[0].wait()
     proj = jnp.dot(res[...], table, preferred_element_type=F32).astype(BF16)
-
-    blocks = route[0].astype(F32)
-    listed = blocks.astype(BF16)
-    owner = (iota((K, NS), 0) >> 2) == iota((K, NS), 1)
-    spread = lax.dot_general(
-        owner.astype(F32).astype(BF16), listed, (((1,), (1,)), ((), ())), preferred_element_type=F32
-    )
-    q = iota((K, 1), 0) & 3
-    block = jnp.where(q < 2, spread[:, 0:1], spread[:, 1:2])
-    want = 2.0 * block + (q & 1).astype(F32)
-    pick = (iota((K, 384), 1).astype(F32) == want).astype(F32).astype(BF16)
     tile = jnp.dot(pick, proj, preferred_element_type=F32)
     snd[...] = tile.astype(BF16).reshape(NS, ROWS, 128)
-    flags = jnp.where(blocks >= 0.0, 1.0, 0.0)
-    flags = jnp.concatenate([flags, jnp.zeros((2, 128 - NS), F32)], axis=1)
-    mrcv[pl.ds(k, 1), pl.ds(z, 1)] = flags.astype(BF16).reshape(1, 1, 2, 128)
 
     pl.semaphore_wait(bar, NS - 1 + NV - 1)
 
@@ -178,64 +180,76 @@
             wgt[pl.ds(d * CHUNK + m * SHARE, SHARE), :] = w.astype(BF16)
     forward_marks()
 
-    drain(mrcv.at[pl.ds(0, 7)], mr2)
-    here = (iota((128, 128), 0) == s).astype(F32).astype(BF16)
-    marks = jnp.dot(mrcv[...].reshape(2 * NS, 128), here, preferred_element_type=F32).astype(BF16)
+    slots = []
+    for b in range(16):
+        slot = jnp.int32(MB)
+        for m in range(MB):
+            slot = jnp.where(occ[0, m] == b, m, slot)
+        slots.append(slot)
     r = iota((K, 1), 0)
     a = r >> 2
     xa = (a >= 24).astype(jnp.int32) + (a >= 48).astype(jnp.int32) + (a >= 72).astype(jnp.int32)
     place = 24 * (2 * xa + (a & 1)) + 2 * ((a - 24 * xa) >> 1) + ((r >> 1) & 1)
     twice = (place == iota((K, 2 * NS), 1)).astype(F32).astype(BF16)
-    marks = jnp.dot(twice, marks, preferred_element_type=F32).astype(BF16)
+    here = (iota((128, 128), 0) == s).astype(F32).astype(BF16)
+    diag = iota((128, 128), 0) == iota((128, 128), 1)
+    fetch[6].wait()
 
     drain(rcv.at[pl.ds(0, NS - 1)], rs)
     rcv[pl.ds(s, 1)] = snd[pl.ds(s, 1)]
-    both = jnp.concatenate([rcv[...].reshape(K, 128), marks], axis=1)
-    diag = iota((128, 128), 0) == iota((128, 128), 1)
-
-    def chunk(d):
-        r = jnp.dot(wgt[pl.ds(pl.multiple_of(d * CHUNK, CHUNK), CHUNK), :], both, preferred_element_type=F32)
-        ray = jnp.sum(jnp.where(diag, r[:, 128:], 0.0), axis=0, keepdims=True)
-        return r[:, :128], ray
+    rows = rcv[...].reshape(K, 128)
+
+    def chunk(d, right):
+        left = wgt[pl.ds(pl.multiple_of(d * CHUNK, CHUNK), CHUNK), :]
+        return jnp.dot(left, right, preferred_element_type=F32)
 
     for d in (4, 3, 5, 2, 6, 1, 7):
         t = (y + d) & 7
-        num, ray = chunk(t)
+        part[t] = chunk(t, rows).astype(BF16)
+        pltpu.make_async_remote_copy(
+            src_ref=part.at[t], dst_ref=got.at[y], send_sem=ss2, recv_sem=rs2.at[y],
+            device_id=(s, t), device_id_type=MESH,
+        ).start()
+
+    drain(mrcv.at[pl.ds(0, 7)], mr2)
+    marks = jnp.dot(mrcv[...].reshape(2 * NS, 128), here, preferred_element_type=F32).astype(BF16)
+    marks = jnp.dot(twice, marks, preferred_element_type=F32).astype(BF16)
+
+    def ray_of(d):
+        return jnp.sum(jnp.where(diag, chunk(d, marks), 0.0), axis=0, keepdims=True)
+
+    for d in (4, 3, 5, 2, 6, 1, 7):
+        t = (y + d) & 7
+        ray = ray_of(t)
         hi = ray.astype(BF16)
         lo = (ray - hi.astype(F32)).astype(BF16)
-        part[t] = num.astype(BF16)
         hilo = jnp.concatenate([hi.astype(F32), lo.astype(F32)], axis=0)
         rpart[pl.ds(t, 1)] = hilo.astype(BF16).reshape(1, 2, 128)
-        pltpu.make_async_remote_copy(
-            src_ref=part.at[t], dst_ref=got.at[y], send_sem=ss2, recv_sem=rs2,
-            device_id=(s, t), device_id_type=MESH,
-        ).start()
         pltpu.make_async_remote_copy(
             src_ref=rpart.at[t], dst_ref=rgot.at[y], send_sem=ss3, recv_sem=rs3,
             device_id=(s, t), device_id_type=MESH,
         ).start()
-    num, ray = chunk(y)
-    got[pl.ds(y, 1)] = jnp.zeros((1, CHUNK, 128), BF16)
+
+    num = chunk(y, rows)
+    ray = ray_of(y)
+    upd[MB:MB + 1] = jnp.zeros((1, SHARE, 128), F32)
     rgot[pl.ds(y, 1)] = jnp.zeros((1, 2, 128), BF16)
-    fetch[6].wait()
     drain(snd.at[pl.ds(0, NS - 1)], ss)
     drain(mrcv.at[0, pl.ds(0, 11)], ms)
     drain(mrcv.at[pl.ds(0, 7)], ms2)
+    for d in (1, 7, 2, 6, 3, 5, 4):
+        v = (y + d) & 7
+        drain(got.at[v], rs2.at[v])
+        num = num + got[v].astype(F32)
     drain(rgot.at[pl.ds(0, NV - 1)], rs3)
-    drain(got.at[pl.ds(0, NV - 1)], rs2)
     for v in range(NV):
-        num = num + got[v].astype(F32)
         tail = rgot[v].astype(F32)
         ray = ray + (tail[0:1] + tail[1:2])
     rayc = jnp.broadcast_to(ray, (128, 128)).T
     new = RELAX * num / (rayc + SHIFT)
     upd[0:MB] = new.reshape(MB, SHARE, 128)
-    upd[MB:MB + 1] = jnp.zeros((1, SHARE, 128), F32)
     for b in range(16):
-        slot = jnp.int32(MB)
-        for m in range(MB):
-            slot = jnp.where(occ[0, m] == b, m, slot)
-        out[b] = vol[b] + upd[slot]
+        out[b] = vol[b] + upd[slots[b]]
     drain(part.at[pl.ds(0, NV - 1)], ss2)
     drain(rpart.at[pl.ds(0, NV - 1)], ss3)
 
@@ -265,7 +279,7 @@
             pltpu.VMEM((NV, 2, 128), BF16),
             pltpu.VMEM((NV, 2, 128), BF16),
             pltpu.VMEM((MB + 1, SHARE, 128), F32),
-            sem((7,)), sem, sem, sem, sem, sem, sem, sem, sem, sem, sem,
+            sem((7,)), sem, sem, sem, sem, sem, sem, sem, sem((NV,)), sem, sem,
         ],
         compiler_params=pltpu.CompilerParams(
             collective_id=0, has_side_effects=True, vmem_limit_bytes=60 << 20

time: 40 us -> 40.9 us (1.022)
  Pallas kernels: 38.3 us -> 39.2 us
    pallas_call x1, Pallas kernels: 38.3 us -> 39.2 us  [per_device(): pl.pallas_call(body, out_shape=jax.ShapeDtypeStruct(volume.shape, F32), i...]
where the time goes in v4:
time: 40.9 us; the launch traced here: 40.8 us
  Pallas kernels  39.2 us (96%)
  local copies, waits for them, and re-layouts  1.57 us (4%)
    pallas_call x1, Pallas kernels, per_device(): pl.pallas_call(body, out_shape=jax.ShapeDtypeStruct(volume.shape, F32), i...  39.2 us
    unnamed x1, local copies, waits for them, and re-layouts  1.57 us

profile of v4, /device:TPU:1, one launch (start us, length us, event | category | flops | bytes accessed | tf_op | source)
XLA Modules:
  0.0 40.8 jit_solution(13135881840578058320)
XLA Ops:
  0.0 39.2 %shard_map.73 = f32[16,16,128]{2,1,0:T(8,128)} custom-call(s32[768]{0:T(1024)} %offs_h.1, s32[1,8]{1,0:T(1,128)} %occ_h.1, bf16[384,128]{1,0:T(8,128)(2,1)} %bitcast.2, s32[1,2,96]{2,1,0:T(2,128)} %bitcast.3, f32[4,768]{1,0:T(4,128)} %geo_h.1, f32[2,16,128]{2,1,0:T(8,128)} %lines_h.1, f32[16,16,128]{2,1,0:T(8,128)} %vol_h.1), custom_call_target="tpu_custom_call" | custom-call | tf_op jit(solution)/shard_map/pallas_call | solution.py:260
  39.2 1.6 %copy.9 = f32[16,16,128]{2,1,0:T(8,128)} copy(f32[16,16,128]{2,1,0:T(8,128)} %shard_map.73) | data formatting | bytes 262144

commit v5 on v3

--- a/solution.py
+++ b/solution.py
@@ -34,22 +34,27 @@
     return jnp.where(t >= n, t - n, t)
 
 
-def peers(s, act):
+def peers(s, act, twin=None):
     x = s // 24
     z = (s - 24 * x) >> 1
     c = s & 1
-    bases = [24 * ((x + dx) & 3) + (c ^ dc) for dx in (2, 1, 3, 0) for dc in (1, 0)]
+    bases = [(dc, 24 * ((x + dx) & 3) + (c ^ dc)) for dx in (2, 1, 3, 0) for dc in (0, 1)]
+
+    def visit(dc, p):
+        if twin is not None and dc == 0:
+            twin(p)
+        act(p)
 
     def column(i, carry):
-        dz = jnp.where(i >= 6, i - 5, i + 6)
+        dz = 6 + ((i + 1) >> 1) * (1 - 2 * (i & 1))
         t = 2 * ring(z, dz, 12)
-        for base in bases:
-            act(base + t)
+        for dc, base in bases:
+            visit(dc, base + t)
         return carry
 
     lax.fori_loop(0, 11, column, 0)
-    for base in bases[:-1]:
-        act(base + 2 * z)
+    for dc, base in bases[:6] + bases[7:]:
+        visit(dc, base + 2 * z)
 
 
 def body(
@@ -63,7 +68,7 @@
     x = s // 24
     z = (s - 24 * x) >> 1
     core = s & 1
-    k = 2 * x + core
+    chip = s >> 1
 
     fetch = [
         pltpu.make_async_copy(h, v, ins.at[i])
@@ -112,20 +117,9 @@
     snd[...] = tile.astype(BF16).reshape(NS, ROWS, 128)
     flags = jnp.where(blocks >= 0.0, 1.0, 0.0)
     flags = jnp.concatenate([flags, jnp.zeros((2, 128 - NS), F32)], axis=1)
-    mrcv[pl.ds(k, 1), pl.ds(z, 1)] = flags.astype(BF16).reshape(1, 1, 2, 128)
+    mrcv[pl.ds(core, 1), pl.ds(chip, 1)] = flags.astype(BF16).reshape(1, 1, 2, 128)
 
     pl.semaphore_wait(bar, NS - 1 + NV - 1)
-
-    def send_marks(i, c):
-        dz = jnp.where(i >= 6, i - 5, i + 6)
-        t = ring(z, dz, 12)
-        pltpu.make_async_remote_copy(
-            src_ref=mrcv.at[k, z], dst_ref=mrcv.at[k, z], send_sem=ms, recv_sem=mr,
-            device_id=(24 * x + 2 * t + core, y), device_id_type=MESH,
-        ).start()
-        return c
-
-    lax.fori_loop(0, 11, send_marks, 0)
 
     def send(p):
         pltpu.make_async_remote_copy(
@@ -133,7 +127,13 @@
             device_id=(p, y), device_id_type=MESH,
         ).start()
 
-    peers(s, send)
+    def send_marks(p):
+        pltpu.make_async_remote_copy(
+            src_ref=mrcv.at[core, chip], dst_ref=mrcv.at[core, chip], send_sem=ms, recv_sem=mr,
+            device_id=(p, y), device_id_type=MESH,
+        ).start()
+
+    peers(s, send, send_marks)
 
     for f in fetch[4:6]:
         f.wait()
@@ -153,13 +153,11 @@
     sweep = 1.2 * gg[2:3] - 0.6
     level = (iota((1, K), 1) & 3).astype(F32)
     def forward_marks():
-        drain(mrcv.at[0, pl.ds(0, 11)], mr)
-        for dx, dc in ((2, 1), (2, 0), (1, 1), (3, 1), (1, 0), (3, 0), (0, 1)):
-            p = 24 * ((x + dx) & 3) + 2 * z + (core ^ dc)
-            pltpu.make_async_remote_copy(
-                src_ref=mrcv.at[k], dst_ref=mrcv.at[k], send_sem=ms2, recv_sem=mr2,
-                device_id=(p, y), device_id_type=MESH,
-            ).start()
+        drain(mrcv.at[0, pl.ds(0, 47)], mr)
+        pltpu.make_async_remote_copy(
+            src_ref=mrcv.at[core], dst_ref=mrcv.at[core], send_sem=ms2, recv_sem=mr2,
+            device_id=(s ^ 1, y), device_id_type=MESH,
+        ).start()
 
     hs = []
     ds = []
@@ -178,13 +176,12 @@
             wgt[pl.ds(d * CHUNK + m * SHARE, SHARE), :] = w.astype(BF16)
     forward_marks()
 
-    drain(mrcv.at[pl.ds(0, 7)], mr2)
+    drain(mrcv.at[0], mr2)
     here = (iota((128, 128), 0) == s).astype(F32).astype(BF16)
     marks = jnp.dot(mrcv[...].reshape(2 * NS, 128), here, preferred_element_type=F32).astype(BF16)
     r = iota((K, 1), 0)
     a = r >> 2
-    xa = (a >= 24).astype(jnp.int32) + (a >= 48).astype(jnp.int32) + (a >= 72).astype(jnp.int32)
-    place = 24 * (2 * xa + (a & 1)) + 2 * ((a - 24 * xa) >> 1) + ((r >> 1) & 1)
+    place = 96 * (a & 1) + 2 * (a >> 1) + ((r >> 1) & 1)
     twice = (place == iota((K, 2 * NS), 1)).astype(F32).astype(BF16)
     marks = jnp.dot(twice, marks, preferred_element_type=F32).astype(BF16)
 
@@ -219,8 +216,8 @@
     rgot[pl.ds(y, 1)] = jnp.zeros((1, 2, 128), BF16)
     fetch[6].wait()
     drain(snd.at[pl.ds(0, NS - 1)], ss)
-    drain(mrcv.at[0, pl.ds(0, 11)], ms)
-    drain(mrcv.at[pl.ds(0, 7)], ms2)
+    drain(mrcv.at[0, pl.ds(0, 47)], ms)
+    drain(mrcv.at[0], ms2)
     drain(rgot.at[pl.ds(0, NV - 1)], rs3)
     drain(got.at[pl.ds(0, NV - 1)], rs2)
     for v in range(NV):
@@ -258,7 +255,7 @@
             pltpu.VMEM((16, SHARE, 128), F32),
             pltpu.VMEM((NS, ROWS, 128), BF16),
             pltpu.VMEM((NS, ROWS, 128), BF16),
-            pltpu.VMEM((8, 12, 2, 128), BF16),
+            pltpu.VMEM((2, 48, 2, 128), BF16),
             pltpu.VMEM((NV * CHUNK, K), BF16),
             pltpu.VMEM((NV, CHUNK, 128), BF16),
             pltpu.VMEM((NV, CHUNK, 128), BF16),

time: 40 us -> 40.4 us (1.010)
  no operation moved by 1% of the time
where the time goes in v5:
time: 40.4 us; the launch traced here: 40.3 us
  Pallas kernels  38.7 us (96%)
  local copies, waits for them, and re-layouts  1.57 us (4%)
    pallas_call x1, Pallas kernels, per_device(): pl.pallas_call(body, out_shape=jax.ShapeDtypeStruct(volume.shape, F32), i...  38.7 us
    unnamed x1, local copies, waits for them, and re-layouts  1.57 us

profile of v5, /device:TPU:1, one launch (start us, length us, event | category | flops | bytes accessed | tf_op | source)
XLA Modules:
  0.0 40.3 jit_solution(13124284659732777509)
XLA Ops:
  0.0 38.7 %shard_map.73 = f32[16,16,128]{2,1,0:T(8,128)} custom-call(s32[768]{0:T(1024)} %offs_h.1, s32[1,8]{1,0:T(1,128)} %occ_h.1, bf16[384,128]{1,0:T(8,128)(2,1)} %bitcast.2, s32[1,2,96]{2,1,0:T(2,128)} %bitcast.3, f32[4,768]{1,0:T(4,128)} %geo_h.1, f32[2,16,128]{2,1,0:T(8,128)} %lines_h.1, f32[16,16,128]{2,1,0:T(8,128)} %vol_h.1), custom_call_target="tpu_custom_call" | custom-call | tf_op jit(solution)/shard_map/pallas_call | solution.py:243
  38.7 1.6 %copy.9 = f32[16,16,128]{2,1,0:T(8,128)} copy(f32[16,16,128]{2,1,0:T(8,128)} %shard_map.73) | data formatting | bytes 262144

commit v6 on v4

--- a/solution.py
+++ b/solution.py
@@ -41,7 +41,7 @@
     bases = [24 * ((x + dx) & 3) + (c ^ dc) for dx in (2, 1, 3, 0) for dc in (1, 0)]
 
     def column(i, carry):
-        dz = jnp.where(i >= 6, i - 5, i + 6)
+        dz = 6 + ((i + 1) >> 1) * (1 - 2 * (i & 1))
         t = 2 * ring(z, dz, 12)
         for base in bases:
             act(base + t)
@@ -55,7 +55,7 @@
 def body(
     offs_h, occ_h, res_h, route_h, geo_h, lines_h, vol_h, out,
     offs, occ, res, route, geo, lines, vol,
-    snd, rcv, mrcv, wgt, part, got, rpart, rgot, upd, ins, ss, rs, ms, mr, ms2, mr2, ss2, rs2, ss3, rs3,
+    full, outs, snd, rcv, mrcv, wgt, part, got, rpart, rgot, upd, ins, ss, rs, ms, mr, ms2, mr2, ss2, rs2, ss3, rs3,
 ):
     s = lax.axis_index("slab")
     y = lax.axis_index("view")
@@ -119,7 +119,7 @@
     pl.semaphore_wait(bar, NS - 1 + NV - 1)
 
     def send_marks(i, c):
-        dz = jnp.where(i >= 6, i - 5, i + 6)
+        dz = 6 + ((i + 1) >> 1) * (1 - 2 * (i & 1))
         t = ring(z, dz, 12)
         pltpu.make_async_remote_copy(
             src_ref=mrcv.at[k, z], dst_ref=mrcv.at[k, z], send_sem=ms, recv_sem=mr,
@@ -186,54 +186,46 @@
         for m in range(MB):
             slot = jnp.where(occ[0, m] == b, m, slot)
         slots.append(slot)
+
+    drain(mrcv.at[pl.ds(0, 7)], mr2)
+    here = (iota((128, 128), 0) == s).astype(F32).astype(BF16)
+    marks = jnp.dot(mrcv[...].reshape(2 * NS, 128), here, preferred_element_type=F32).astype(BF16)
     r = iota((K, 1), 0)
     a = r >> 2
     xa = (a >= 24).astype(jnp.int32) + (a >= 48).astype(jnp.int32) + (a >= 72).astype(jnp.int32)
     place = 24 * (2 * xa + (a & 1)) + 2 * ((a - 24 * xa) >> 1) + ((r >> 1) & 1)
     twice = (place == iota((K, 2 * NS), 1)).astype(F32).astype(BF16)
-    here = (iota((128, 128), 0) == s).astype(F32).astype(BF16)
-    diag = iota((128, 128), 0) == iota((128, 128), 1)
-    fetch[6].wait()
+    marks = jnp.dot(twice, marks, preferred_element_type=F32).astype(BF16)
 
     drain(rcv.at[pl.ds(0, NS - 1)], rs)
     rcv[pl.ds(s, 1)] = snd[pl.ds(s, 1)]
-    rows = rcv[...].reshape(K, 128)
-
-    def chunk(d, right):
-        left = wgt[pl.ds(pl.multiple_of(d * CHUNK, CHUNK), CHUNK), :]
-        return jnp.dot(left, right, preferred_element_type=F32)
+    both = jnp.concatenate([rcv[...].reshape(K, 128), marks], axis=1)
+    diag = iota((128, 128), 0) == iota((128, 128), 1)
+
+    def chunk(d):
+        r = jnp.dot(wgt[pl.ds(pl.multiple_of(d * CHUNK, CHUNK), CHUNK), :], both, preferred_element_type=F32)
+        ray = jnp.sum(jnp.where(diag, r[:, 128:], 0.0), axis=0, keepdims=True)
+        return r[:, :128], ray
 
     for d in (4, 3, 5, 2, 6, 1, 7):
         t = (y + d) & 7
-        part[t] = chunk(t, rows).astype(BF16)
+        num, ray = chunk(t)
+        hi = ray.astype(BF16)
+        lo = (ray - hi.astype(F32)).astype(BF16)
+        part[t] = num.astype(BF16)
+        hilo = jnp.concatenate([hi.astype(F32), lo.astype(F32)], axis=0)
+        rpart[pl.ds(t, 1)] = hilo.astype(BF16).reshape(1, 2, 128)
         pltpu.make_async_remote_copy(
             src_ref=part.at[t], dst_ref=got.at[y], send_sem=ss2, recv_sem=rs2.at[y],
             device_id=(s, t), device_id_type=MESH,
         ).start()
-
-    drain(mrcv.at[pl.ds(0, 7)], mr2)
-    marks = jnp.dot(mrcv[...].reshape(2 * NS, 128), here, preferred_element_type=F32).astype(BF16)
-    marks = jnp.dot(twice, marks, preferred_element_type=F32).astype(BF16)
-
-    def ray_of(d):
-        return jnp.sum(jnp.where(diag, chunk(d, marks), 0.0), axis=0, keepdims=True)
-
-    for d in (4, 3, 5, 2, 6, 1, 7):
-        t = (y + d) & 7
-        ray = ray_of(t)
-        hi = ray.astype(BF16)
-        lo = (ray - hi.astype(F32)).astype(BF16)
-        hilo = jnp.concatenate([hi.astype(F32), lo.astype(F32)], axis=0)
-        rpart[pl.ds(t, 1)] = hilo.astype(BF16).reshape(1, 2, 128)
         pltpu.make_async_remote_copy(
             src_ref=rpart.at[t], dst_ref=rgot.at[y], send_sem=ss3, recv_sem=rs3,
             device_id=(s, t), device_id_type=MESH,
         ).start()
-
-    num = chunk(y, rows)
-    ray = ray_of(y)
-    upd[MB:MB + 1] = jnp.zeros((1, SHARE, 128), F32)
+    num, ray = chunk(y)
     rgot[pl.ds(y, 1)] = jnp.zeros((1, 2, 128), BF16)
+    fetch[6].wait()
     drain(snd.at[pl.ds(0, NS - 1)], ss)
     drain(mrcv.at[0, pl.ds(0, 11)], ms)
     drain(mrcv.at[pl.ds(0, 7)], ms2)
@@ -248,10 +240,18 @@
     rayc = jnp.broadcast_to(ray, (128, 128)).T
     new = RELAX * num / (rayc + SHIFT)
     upd[0:MB] = new.reshape(MB, SHARE, 128)
+    upd[MB:MB + 1] = jnp.zeros((1, SHARE, 128), F32)
+    stores = []
     for b in range(16):
-        out[b] = vol[b] + upd[slots[b]]
+        full[b] = vol[b] + upd[slots[b]]
+        if b % 4 == 3:
+            span = pl.ds(b - 3, 4)
+            stores.append(pltpu.make_async_copy(full.at[span], out.at[span], outs.at[b // 4]))
+            stores[-1].start()
     drain(part.at[pl.ds(0, NV - 1)], ss2)
     drain(rpart.at[pl.ds(0, NV - 1)], ss3)
+    for f in stores:
+        f.wait()
 
 
 def per_device(residual, route_list, tile_offsets, view_geometry, line_coords, occupied, volume):
@@ -261,7 +261,7 @@
         body,
         out_shape=jax.ShapeDtypeStruct(volume.shape, F32),
         in_specs=[hbm] * 7,
-        out_specs=pl.BlockSpec(memory_space=pltpu.VMEM),
+        out_specs=hbm,
         scratch_shapes=[
             pltpu.SMEM((VIEWS,), jnp.int32),
             pltpu.SMEM((1, MB), jnp.int32),
@@ -270,6 +270,8 @@
             pltpu.VMEM((4, VIEWS), F32),
             pltpu.VMEM((2, 16, 128), F32),
             pltpu.VMEM((16, SHARE, 128), F32),
+            pltpu.VMEM((16, SHARE, 128), F32),
+            sem((4,)),
             pltpu.VMEM((NS, ROWS, 128), BF16),
             pltpu.VMEM((NS, ROWS, 128), BF16),
             pltpu.VMEM((8, 12, 2, 128), BF16),

time: 40.9 us -> 40.1 us (0.980)
  Pallas kernels: 39.2 us -> 38.4 us
    pallas_call x1, Pallas kernels: 39.2 us -> 38.4 us  [per_device(): pl.pallas_call(body, out_shape=jax.ShapeDtypeStruct(volume.shape, F32), i...]
where the time goes in v6:
time: 40.1 us; the launch traced here: 40 us
  Pallas kernels  38.4 us (96%)
  local copies, waits for them, and re-layouts  1.57 us (4%)
    pallas_call x1, Pallas kernels, per_device(): pl.pallas_call(body, out_shape=jax.ShapeDtypeStruct(volume.shape, F32), i...  38.4 us
    unnamed x1, local copies, waits for them, and re-layouts  1.57 us

profile of v6, /device:TPU:1, one launch (start us, length us, event | category | flops | bytes accessed | tf_op | source)
XLA Modules:
  0.0 40.0 jit_solution(5915026738340677345)
XLA Ops:
  0.0 38.4 %shard_map.73 = f32[16,16,128]{2,1,0:T(8,128)} custom-call(s32[768]{0:T(1024)} %offs_h.1, s32[1,8]{1,0:T(1,128)} %occ_h.1, bf16[384,128]{1,0:T(8,128)(2,1)} %bitcast.2, s32[1,2,96]{2,1,0:T(2,128)} %bitcast.3, f32[4,768]{1,0:T(4,128)} %geo_h.1, f32[2,16,128]{2,1,0:T(8,128)} %lines_h.1, f32[16,16,128]{2,1,0:T(8,128)} %vol_h.1), custom_call_target="tpu_custom_call" | custom-call | tf_op jit(solution)/shard_map/pallas_call | solution.py:260
  38.4 1.6 %copy.9 = f32[16,16,128]{2,1,0:T(8,128)} copy(f32[16,16,128]{2,1,0:T(8,128)} %shard_map.73) | data formatting | bytes 262144

commit v7 on v3

--- a/solution.py
+++ b/solution.py
@@ -41,7 +41,7 @@
     bases = [24 * ((x + dx) & 3) + (c ^ dc) for dx in (2, 1, 3, 0) for dc in (1, 0)]
 
     def column(i, carry):
-        dz = jnp.where(i >= 6, i - 5, i + 6)
+        dz = 6 + ((i + 1) >> 1) * (1 - 2 * (i & 1))
         t = 2 * ring(z, dz, 12)
         for base in bases:
             act(base + t)
@@ -117,7 +117,7 @@
     pl.semaphore_wait(bar, NS - 1 + NV - 1)
 
     def send_marks(i, c):
-        dz = jnp.where(i >= 6, i - 5, i + 6)
+        dz = 6 + ((i + 1) >> 1) * (1 - 2 * (i & 1))
         t = ring(z, dz, 12)
         pltpu.make_async_remote_copy(
             src_ref=mrcv.at[k, z], dst_ref=mrcv.at[k, z], send_sem=ms, recv_sem=mr,

time: 40 us -> 40 us (level)
  no operation moved by 1% of the time
where the time goes in v7:
time: 40 us; the launch traced here: 39.9 us
  Pallas kernels  38.3 us (96%)
  local copies, waits for them, and re-layouts  1.57 us (4%)
    pallas_call x1, Pallas kernels, per_device(): pl.pallas_call(body, out_shape=jax.ShapeDtypeStruct(volume.shape, F32), i...  38.3 us
    unnamed x1, local copies, waits for them, and re-layouts  1.57 us

profile of v7, /device:TPU:1, one launch (start us, length us, event | category | flops | bytes accessed | tf_op | source)
XLA Modules:
  0.0 39.9 jit_solution(17549192700590578317)
XLA Ops:
  0.0 38.3 %shard_map.73 = f32[16,16,128]{2,1,0:T(8,128)} custom-call(s32[768]{0:T(1024)} %offs_h.1, s32[1,8]{1,0:T(1,128)} %occ_h.1, bf16[384,128]{1,0:T(8,128)(2,1)} %bitcast.2, s32[1,2,96]{2,1,0:T(2,128)} %bitcast.3, f32[4,768]{1,0:T(4,128)} %geo_h.1, f32[2,16,128]{2,1,0:T(8,128)} %lines_h.1, f32[16,16,128]{2,1,0:T(8,128)} %vol_h.1), custom_call_target="tpu_custom_call" | custom-call | tf_op jit(solution)/shard_map/pallas_call | solution.py:246
  38.3 1.6 %copy.9 = f32[16,16,128]{2,1,0:T(8,128)} copy(f32[16,16,128]{2,1,0:T(8,128)} %shard_map.73) | data formatting | bytes 262144
